TPU v7x, 256 devices: a whole 4x4x8 slice. The times are simulated.
256 devices in a mesh: ctx: 32 (over z_hi, x, y), tp: 8 (over z_lo, core).
Axes of the slice: x: 4, y: 4, z: 8 (z_hi: 2, z_lo: 4; z = z_hi * 4 + z_lo), core: 2. Of those that a mesh axis runs over, the one named last changes fastest.
Arguments:
- hidden: bfloat16 [16384, 4096], P('ctx', 'tp'), may hold values from -6 to 6
- norm_gain: float32 [4096], replicated, may hold values from 0.5 to 10
- w_query: bfloat16 [4096, 4096], P('ctx', 'tp'), may hold values from -0.09375 to 0.09375
- w_key: bfloat16 [4096, 512], P('ctx'), may hold values from -0.09375 to 0.09375
- w_value: bfloat16 [4096, 512], P('ctx'), may hold values from -0.09375 to 0.09375
- w_out: bfloat16 [4096, 4096], P('tp', 'ctx'), may hold values from -0.09375 to 0.09375
- kept_rows: int32 [32, 320], replicated, may hold values from 0 to 511, as said below
- kept_count: int32 [32], replicated, may hold values from 192 to 320, as said below
Outputs:
- layer_out: bfloat16 [16384, 4096], P('ctx', 'tp')
Inputs may be any that keep to these rules, and one draw needn't show every extreme that they name: `kept_rows`: each row is sorted; its first kept_count entries are distinct and increasing, and the entries after them repeat the last kept one. `kept_count`: some shard keeps exactly 320 positions.
All inputs are finite; a program needn't handle non-finite values.
Results may differ from a plain program's by a relative error of at most 0.019.
The roundings to bfloat16 on the way count: a program that leaves them out, or rounds other values in their place, can miss the bound.
Values may be sent and summed in bfloat16 or wider, within the bound.
No kernel may reach another device: no remote copies, remote signals or barrier semaphores. Data moves between devices by JAX's collectives and lax.ppermute only.
A program may use at most 64 MiB of HBM per device.

v0:
```python
import math

import jax
import jax.numpy as jnp
from jax import lax
from jax.sharding import PartitionSpec as P

Q_HEADS = 32
KV_HEADS = 4
HEAD_DIM = 128


EPSILON = 1e-05
ROPE_BASE = 10000.0


def rms_rows(rows, norm_gain):
    values = rows.astype(jnp.float32)
    spread = jnp.mean(values * values, axis=-1, keepdims=True)
    return (values * lax.rsqrt(spread + EPSILON) * norm_gain).astype(jnp.bfloat16)


def rotary(vectors, positions):
    head_width = vectors.shape[-1]
    halfway = head_width // 2
    exponent = jnp.arange(halfway, dtype=jnp.float32) * (2.0 / head_width)
    inverse = jnp.exp(-math.log(ROPE_BASE) * exponent)
    angles = positions.astype(jnp.float32)[:, None] * inverse[None, :]
    cosine = jnp.cos(angles)[:, None, :]
    sine_part = jnp.sin(angles)[:, None, :]
    first_half = vectors[..., :halfway]
    second = vectors[..., halfway:]
    return jnp.concatenate(
        [first_half * cosine - second * sine_part, second * cosine + first_half * sine_part],
        axis=-1,
    )


def attend(queries, query_pos, all_keys, all_values, key_pos, key_live, key_block, block_count):
    row_count, kv_local, group_local, head_width = queries.shape
    score_scale = 1.0 / math.sqrt(head_width)

    def accumulate(block_index, carried):
        summed, row_total, row_peak = carried
        first_key = block_index * key_block
        key_piece = lax.dynamic_slice_in_dim(all_keys, first_key, key_block, 0)
        value_piece = lax.dynamic_slice_in_dim(all_values, first_key, key_block, 0)
        piece_pos = lax.dynamic_slice_in_dim(key_pos, first_key, key_block, 0)
        piece_live = lax.dynamic_slice_in_dim(key_live, first_key, key_block, 0)
        scores = (
            jnp.einsum("rhgd,khd->rhgk", queries, key_piece, preferred_element_type=jnp.float32)
            * score_scale
        )
        allowed = (piece_live[None, :] & (piece_pos[None, :] <= query_pos[:, None]))[
            :, None, None, :
        ]
        new_peak = jnp.maximum(row_peak, jnp.max(jnp.where(allowed, scores, -1e30), axis=-1))
        rescale = jnp.exp(row_peak - new_peak)
        weights = jnp.where(allowed, jnp.exp(scores - new_peak[..., None]), 0.0)
        summed = summed * rescale[..., None] + jnp.einsum(
            "rhgk,khd->rhgd",
            weights.astype(jnp.bfloat16),
            value_piece,
            preferred_element_type=jnp.float32,
        )
        row_total = row_total * rescale + jnp.sum(weights, axis=-1)
        return (summed, row_total, new_peak)

    start_sums = (
        jnp.zeros((row_count, kv_local, group_local, head_width), jnp.float32),
        jnp.zeros((row_count, kv_local, group_local), jnp.float32),
        jnp.full((row_count, kv_local, group_local), -1e30, jnp.float32),
    )
    summed, row_total, unused_peak = lax.fori_loop(0, block_count, accumulate, start_sums)
    return (
        (summed / row_total[..., None])
        .astype(jnp.bfloat16)
        .reshape(row_count, kv_local * group_local * head_width)
    )


def per_device(hidden, norm_gain, w_query, w_key, w_value, w_out, kept_rows, kept_count):
    shards = lax.axis_size("ctx")
    ctx_index = lax.axis_index("ctx")
    tp_index = lax.axis_index("tp")
    capacity = kept_rows.shape[1]
    per_shard = hidden.shape[0]
    local_heads = w_query.shape[1] // HEAD_DIM
    group_size = Q_HEADS // KV_HEADS
    group_local = min(local_heads, group_size)
    kv_local = local_heads // group_local
    kv_first = tp_index * local_heads // group_size
    offsets = (jnp.arange(shards, dtype=jnp.int32) * per_shard)[:, None]
    position_table = offsets + kept_rows
    key_pos = position_table.reshape(-1)
    key_live = (jnp.arange(capacity, dtype=jnp.int32)[None, :] < kept_count[:, None]).reshape(-1)
    own_rows = lax.dynamic_index_in_dim(kept_rows, ctx_index, 0, keepdims=False)
    own_pos = lax.dynamic_index_in_dim(position_table, ctx_index, 0, keepdims=False)
    own_count = lax.dynamic_index_in_dim(kept_count, ctx_index, 0, keepdims=False)
    picked = hidden[own_rows]
    features = lax.all_gather(picked, "tp", axis=1, tiled=True)
    normed = rms_rows(features, norm_gain)
    key_cols = lax.dynamic_slice_in_dim(w_key, kv_first * HEAD_DIM, kv_local * HEAD_DIM, 1)
    value_cols = lax.dynamic_slice_in_dim(w_value, kv_first * HEAD_DIM, kv_local * HEAD_DIM, 1)
    pieces = (
        lax.all_gather(w_query, "ctx", axis=0, tiled=True),
        lax.all_gather(key_cols, "ctx", axis=0, tiled=True),
        lax.all_gather(value_cols, "ctx", axis=0, tiled=True),
    )
    query_sum, key_sum, value_sum = tuple(
        (
            jnp.dot(normed, weight_piece, preferred_element_type=jnp.float32)
            for weight_piece in pieces
        )
    )
    queries = rotary(query_sum.reshape(capacity, local_heads, HEAD_DIM), own_pos).astype(
        jnp.bfloat16
    )
    queries = queries.reshape(capacity, kv_local, group_local, HEAD_DIM)
    keys_own = (
        rotary(key_sum.reshape(capacity, kv_local, HEAD_DIM), own_pos)
        .astype(jnp.bfloat16)
        .reshape(capacity, kv_local * HEAD_DIM)
    )
    values_own = value_sum.astype(jnp.bfloat16)
    all_keys, all_values = (
        lax.all_gather(keys_own, "ctx", axis=0, tiled=True),
        lax.all_gather(values_own, "ctx", axis=0, tiled=True),
    )
    all_keys = all_keys.reshape(shards * capacity, kv_local, HEAD_DIM)
    all_values = all_values.reshape(shards * capacity, kv_local, HEAD_DIM)
    key_block = 2 * capacity
    attended = attend(
        queries, own_pos, all_keys, all_values, key_pos, key_live, key_block, ctx_index // 2 + 1
    )
    partial_out = jnp.dot(
        attended,
        lax.all_gather(w_out, "ctx", axis=1, tiled=True),
        preferred_element_type=jnp.float32,
    )
    projected = lax.psum_scatter(
        partial_out.astype(jnp.bfloat16), "tp", scatter_dimension=1, tiled=True
    ).astype(jnp.float32)
    updated = (picked.astype(jnp.float32) + projected).astype(jnp.bfloat16)
    target = jnp.where(jnp.arange(capacity, dtype=jnp.int32) < own_count, own_rows, per_shard)
    return hidden.at[target].set(updated, mode="drop")


def solution(mesh):
    return jax.shard_map(
        per_device,
        mesh=mesh,
        in_specs=(
            P("ctx", "tp"),
            P(),
            P("ctx", "tp"),
            P("ctx", None),
            P("ctx", None),
            P("tp", "ctx"),
            P(),
            P(),
        ),
        out_specs=P("ctx", "tp"),
        check_vma=False,
    )
```

profile of v0, /device:TPU:167, one launch (start us, length us, event | category | flops | bytes accessed | tf_op | source)
XLA Modules:
  0.0 695.7 jit_solution(601102458653337336)
XLA Ops:
  7.6 1.3 dynamic_slice.29
  8.9 1.3 fusion.45
  10.2 2.5 gather_fusion
  13.6 1.4 constant_dynamic-slice_fusion
  15.7 34.3 %all-gather.21.cloned.1.call-done = bf16[320,4096]{1,0:T(8,128)(2,1)} async-done(((bf16[320,512]{1,0:T(8,128)(2,1)}), bf16[320,4096]{1,0:T(8,128)(2,1)}) %all-gather.21.cloned.1.call-update) | async-done | bytes 2621456 | tf_op jit(solution)/shard_map/all_gather | solution.py:101
  50.1 2.3 fusion.26
  52.4 78.5 %all-gather.9.cloned.1.call-done = bf16[4096,128]{1,0:T(8,128)(2,1)} async-done(((bf16[128,128]{1,0:T(8,128)(2,1)}), bf16[4096,128]{1,0:T(8,128)(2,1)}) %all-gather.9.cloned.1.call-update) | async-done | bytes 1048592 | tf_op jit(solution)/shard_map/all_gather | solution.py:107
  130.9 2.9 convolution_bitcast_fusion
  135.4 74.8 %all-gather.15.cloned.1.call-done = bf16[4096,128]{1,0:T(8,128)(2,1)} async-done(((bf16[128,128]{1,0:T(8,128)(2,1)}), bf16[4096,128]{1,0:T(8,128)(2,1)}) %all-gather.15.cloned.1.call-update) | async-done | bytes 1048592 | tf_op jit(solution)/shard_map/all_gather | solution.py:108
  210.2 2.8 convolution_convert_fusion.1
  213.8 1.3 multiply_cosine_fusion
  215.4 105.7 %all-gather.13.cloned.1.call-done = bf16[4096,512]{1,0:T(8,128)(2,1)} async-done(((bf16[128,512]{1,0:T(8,128)(2,1)}), bf16[4096,512]{1,0:T(8,128)(2,1)}) %all-gather.13.cloned.1.call-update) | async-done | bytes 4194320 | tf_op jit(solution)/shard_map/all_gather | solution.py:106
  321.2 4.6 fusion.47
  325.8 1.3 reshape.306
  327.9 85.9 %all-gather.11.cloned.1.call-done = bf16[10240,128]{1,0:T(8,128)(2,1)} async-done(((bf16[320,128]{1,0:T(8,128)(2,1)}), bf16[10240,128]{1,0:T(8,128)(2,1)}) %all-gather.11.cloned.1.call-update) | async-done | bytes 2621456 | tf_op jit(solution)/shard_map/all_gather | solution.py:127
  413.8 93.6 %all-gather.17.cloned.1.call-done = bf16[10240,128]{1,0:T(8,128)(2,1)} async-done(((bf16[320,128]{1,0:T(8,128)(2,1)}), bf16[10240,128]{1,0:T(8,128)(2,1)}) %all-gather.17.cloned.1.call-update) | async-done | bytes 2621456 | tf_op jit(solution)/shard_map/all_gather | solution.py:128
  507.5 83.4 %while.14 = (s32[]{:T(128)}, f32[320,1,4,128]{3,0,2,1:T(8,128)S(1)}, f32[320,1,4]{0,2,1:T(4,128)S(1)}, f32[320,1,4]{0,2,1:T(4,128)S(1)}, s32[]{:T(128)}, /*index...) while((s32[]{:T(128)}, ...), condition=%wide.region_4.5_spmd, body=%wide.region_1.4_spmd.sunk | while | flops 429182720 | bytes 12708683 | solution.py:74
  507.9 1.9 fusion.63
  509.8 1.1 fusion.66
  510.9 2.1 fusion.65
  513.4 1.9 fusion.63
  515.3 1.1 fusion.66
  516.5 2.1 fusion.65
  519.0 1.9 fusion.63
  520.9 1.1 fusion.66
  522.0 2.1 fusion.65
  524.5 1.9 fusion.63
  526.4 1.1 fusion.66
  527.6 2.1 fusion.65
  530.1 1.9 fusion.63
  533.1 2.1 fusion.65
  535.6 1.9 fusion.63
  537.5 1.1 fusion.66
  538.7 2.1 fusion.65
  541.2 1.9 fusion.63
  543.1 1.1 fusion.66
  544.2 2.1 fusion.65
  546.7 1.9 fusion.63
  549.7 2.1 fusion.65
  552.3 1.9 fusion.63
  554.2 1.1 fusion.66
  555.3 2.1 fusion.65
  557.8 1.9 fusion.63
  559.7 1.1 fusion.66
  560.8 2.1 fusion.65
  563.4 1.9 fusion.63
  565.3 1.1 fusion.66
  566.4 2.1 fusion.65
  568.9 1.9 fusion.63
  570.8 1.1 fusion.66
  571.9 2.1 fusion.65
  574.5 1.9 fusion.63
  576.3 1.1 fusion.66
  577.5 2.1 fusion.65
  580.0 1.9 fusion.63
  581.9 1.1 fusion.66
  583.0 2.1 fusion.65
  585.6 1.9 fusion.63
  587.5 1.1 fusion.66
  588.6 2.1 fusion.65
  591.4 49.1 %all-gather.19.cloned.1.call-done = bf16[512,4096]{1,0:T(8,128)(2,1)} async-done(((bf16[512,128]{1,0:T(8,128)(2,1)}), bf16[512,4096]{1,0:T(8,128)(2,1)}) %all-gather.19.cloned.1.call-update) | async-done | bytes 4194320 | tf_op jit(solution)/shard_map/all_gather | solution.py:138
  640.5 5.3 convolution_convert_fusion
  645.8 39.1 %reduce-scatter.2.cloned.1.call-done = bf16[320,512]{1,0:T(8,128)(2,1)} async-done(((bf16[320,4096]{1,0:T(8,128)(2,1)}), bf16[320,512]{1,0:T(8,128)(2,1)}) %reduce-scatter.2.cloned.1.call-update) | async-done | bytes 327696 | tf_op jit(solution)/shard_map/reduce_scatter | solution.py:141
  684.9 4.0 scatter_custom_fusion
  (146 shorter events, 14.6 us)
Async XLA Ops:
  6.5 6.3 copy-start
  6.5 9.1 %copy-start.5 = (s32[32,320]{1,0:T(8,128)S(1)}, s32[32,320]{1,0:T(8,128)}, u32[]{:S(2)}) copy-start(s32[32,320]{1,0:T(8,128)} %param.16) | copy-start | bytes 122884
  6.5 43.5 %all-gather.21.cloned.1.call-start = ((), (), s32[]{:S(2)}) async-start(), calls=%async_computation.8 | async-start | bytes 2949120 | tf_op jit(solution)/shard_map/all_gather | solution.py:101
  7.6 126.3 %copy-start.1 = (bf16[512,512]{1,0:T(8,128)(2,1)}, bf16[512,512]{1,0:T(8,128)(2,1)S(1)}, u32[]{:S(2)}) copy-start(bf16[512,512]{1,0:T(8,128)(2,1)S(1)} %copy.47) | copy-start | bytes 1572868
  7.6 123.3 %copy-start.7 = (f32[4096]{0:T(1024)S(1)}, f32[4096]{0:T(1024)}, u32[]{:S(2)}) copy-start(f32[4096]{0:T(1024)} %param.11) | copy-start | bytes 49156
  12.8 118.2 %all-gather.9.cloned.1.call-start = ((), (), s32[]{:S(2)}) async-start(), calls=%async_computation.1 | async-start | bytes 1081344 | tf_op jit(solution)/shard_map/all_gather | solution.py:107
  13.5 196.7 %all-gather.15.cloned.1.call-start = ((), (), s32[]{:S(2)}) async-start(), calls=%async_computation.4 | async-start | bytes 1081344 | tf_op jit(solution)/shard_map/all_gather | solution.py:108
  15.0 306.2 %all-gather.13.cloned.1.call-start = ((), (), s32[]{:S(2)}) async-start(), calls=%async_computation.3 | async-start | bytes 4325376 | tf_op jit(solution)/shard_map/all_gather | solution.py:106
  15.5 398.3 %all-gather.11.cloned.1.call-start = ((), (), s32[]{:S(2)}) async-start(), calls=%async_computation.2 | async-start | bytes 2703360 | tf_op jit(solution)/shard_map/all_gather | solution.py:127
  52.4 157.8 %copy-start.3 = (bf16[320,4096]{1,0:T(8,128)(2,1)S(1)}, bf16[320,4096]{1,0:T(8,128)(2,1)}, u32[]{:S(2)}) copy-start(bf16[320,4096]{1,0:T(8,128)(2,1)} %all-gather.21.cloned.1.call-done) | copy-start | bytes 7864324
  135.4 79.9 %copy-start.6 = (s32[32]{0:T(128)S(1)}, s32[32]{0:T(128)}, u32[]{:S(2)}) copy-start(s32[32]{0:T(128)} %param.17) | copy-start | bytes 388
  135.4 372.1 %all-gather.17.cloned.1.call-start = ((), (), s32[]{:S(2)}) async-start(), calls=%async_computation.5 | async-start | bytes 2703360 | tf_op jit(solution)/shard_map/all_gather | solution.py:128
  213.0 427.4 %all-gather.19.cloned.1.call-start = ((), (), s32[]{:S(2)}) async-start(), calls=%async_computation.6 | async-start | bytes 4325376 | tf_op jit(solution)/shard_map/all_gather | solution.py:138
  213.8 471.1 %reduce-scatter.2.cloned.1.call-start = ((), (), s32[]{:S(2)}) async-start(), calls=%async_computation.7 | async-start | bytes 2949120 | tf_op jit(solution)/shard_map/reduce_scatter | solution.py:141
  325.8 1.7 copy-start.4
  640.5 44.4 %copy-start.2 = (bf16[320,512]{1,0:T(8,128)(2,1)S(1)}, bf16[320,512]{1,0:T(8,128)(2,1)}, u32[]{:S(2)}) copy-start(bf16[320,512]{1,0:T(8,128)(2,1)} %gather_fusion) | copy-start | bytes 983044
Sparse Core Ops, SparseCore 0:
  12.9 37.1 all-gather.20
  53.5 77.4 all-gather.8
  134.4 75.8 all-gather.14
  213.6 107.5 all-gather.12
  324.5 89.2 all-gather.10
  417.2 90.1 all-gather.16
  510.6 129.8 all-gather.18
  645.9 38.9 reduce-scatter.1
where the time goes:
time: 704 us; the launch traced here: 696 us
  waiting for transfers between devices  562 us (80%)
  matrix products  75.4 us (11%)
  other arithmetic  31.5 us (4%)
  between operations  13.7 us (2%)
  local copies, waits for them, and re-layouts  11.6 us (2%)
    all_gather x1, waiting for transfers between devices, per_device(): lax.all_gather(w_query, 'ctx', axis=0, tiled=True)  106 us
    all_gather x1, waiting for transfers between devices, per_device(): lax.all_gather(values_own, 'ctx', axis=0, tiled=True)  93.6 us
    all_gather x1, waiting for transfers between devices, per_device(): lax.all_gather(keys_own, 'ctx', axis=0, tiled=True)  85.9 us
    all_gather x1, waiting for transfers between devices, per_device(): lax.all_gather(key_cols, 'ctx', axis=0, tiled=True)  78.5 us
    all_gather x1, waiting for transfers between devices, per_device(): lax.all_gather(value_cols, 'ctx', axis=0, tiled=True)  74.8 us
    all_gather x1, waiting for transfers between devices, per_device(): lax.all_gather(w_out, 'ctx', axis=1, tiled=True)  49.1 us
    reduce_scatter x1, waiting for transfers between devices, per_device(): lax.psum_scatter(partial_out.astype(jnp.bfloat16), 'tp', scatter_dimensio...  39.1 us
    all_gather x1, waiting for transfers between devices, per_device(): features = lax.all_gather(picked, 'tp', axis=1, tiled=True)  34.3 us
  transfers between devices with their start and end apart: 8, of which 8 were waited for; matrix products, arithmetic and copies ran while one was open for 15% of the time, Pallas kernels for 0%

commit v1 on v0

v1 whole, which is shorter than its diff:
```python
import functools
import math

import jax
import jax.numpy as jnp
from jax import lax
from jax.experimental import pallas as pl
from jax.experimental.pallas import tpu as pltpu
from jax.sharding import Mesh, PartitionSpec as P

WIDTH = 4096
Q_HEADS = 32
KV_HEADS = 4
HEAD_DIM = 128
EPSILON = 1e-05
ROPE_BASE = 10000.0
LOG2E = math.log2(math.e)
AXES = ("zh", "x", "y", "zl", "c")
SIZES = (2, 4, 4, 4, 2)
BF = jnp.bfloat16
F32 = jnp.float32
VMEM = pl.BlockSpec(memory_space=pltpu.VMEM)
SMEM = pl.BlockSpec(memory_space=pltpu.SMEM)
PARAMS = pltpu.CompilerParams(vmem_limit_bytes=48 * 2**20)


def hop(value, axis, step):
    size = SIZES[AXES.index(axis)]
    return lax.ppermute(value, axis, [(i, (i + step) % size) for i in range(size)])


def hop_mixed(value, first, step):
    pairs = []
    for x in range(4):
        for y in range(4):
            for c in range(2):
                if (c == 0) == first:
                    to = ((x + step) % 4, y)
                else:
                    to = (x, (y + step) % 4)
                pairs.append(((x * 4 + y) * 2 + c, (to[0] * 4 + to[1]) * 2 + c))
    return lax.ppermute(value, ("x", "y", "c"), pairs)


def ring_index(place):
    return lax.bitwise_and(place, 3)


def pick_body(coords, kept_ref, hidden_ref, out_ref):
    ctx = coords[0]
    wanted = kept_ref[pl.ds(ctx, 1), :]
    count = hidden_ref.shape[0]
    cap = wanted.shape[1]
    place = lax.broadcasted_iota(jnp.int32, (count, cap), 0)
    one_hot = (place == wanted).astype(F32).astype(BF)
    out_ref[...] = lax.dot_general(
        one_hot, hidden_ref[...], (((0,), (0,)), ((), ())), preferred_element_type=F32
    ).astype(BF)


def project_body(
    coords, f_ref, g_ref, gain_ref, cos_ref, sin_ref, t0, t1, t2, t3, q_ref, kv_ref, normed
):
    xi, yi, zi, core = coords[1], coords[2], coords[3], coords[4]
    cap = f_ref.shape[1]
    spread = jnp.zeros((cap, HEAD_DIM), F32)
    for ref in (f_ref, g_ref):
        for k in range(4):
            for b in range(4):
                v = ref[k, :, b * 128 : (b + 1) * 128].astype(F32)
                spread = spread + v * v
    scale = lax.rsqrt(jnp.sum(spread, axis=1, keepdims=True) * (1.0 / WIDTH) + EPSILON)
    for ref, side in ((f_ref, core), (g_ref, 1 - core)):
        for k in range(4):
            owner = ring_index(zi - k) * 2 + side
            half = lax.shift_right_logical(owner, 2)
            x = ring_index(owner)
            for y in range(4):
                v = ref[k, :, y * 128 : (y + 1) * 128].astype(F32)
                gain = gain_ref[:, pl.ds(pl.multiple_of(owner * 512 + y * 128, 128), 128)]
                block = jnp.where(core == 0, ring_index(yi - y), ring_index(xi - x))
                column = jnp.where(core == 0, x, y) * 256 + half * 128
                normed[block, :, pl.ds(pl.multiple_of(column, 128), 128)] = (
                    v * scale * gain
                ).astype(BF)
    total = jnp.dot(normed[0], t0[...], preferred_element_type=F32)
    for k, ref in ((1, t1), (2, t2), (3, t3)):
        total = total + jnp.dot(normed[k], ref[...], preferred_element_type=F32)
    cosine = cos_ref[...]
    sine = sin_ref[...]
    heads = q_ref.shape[1] // HEAD_DIM
    for h in range(heads + 1):
        v = total[:, h * HEAD_DIM : (h + 1) * HEAD_DIM]
        turned = pltpu.roll(v, HEAD_DIM // 2, 1)
        if h < heads:
            q_ref[:, h * HEAD_DIM : (h + 1) * HEAD_DIM] = (v * cosine + turned * sine).astype(BF)
        else:
            roped = (v * cosine + turned * sine).astype(BF)
            kv_ref[...] = jnp.where(core == 0, roped, v.astype(BF))


def attend_body(
    kb, coords, counts, q_ref, *refs
):
    k_refs, v_refs = refs[0:4], refs[4:8]
    out_ref, keys, vals, peak_ref, acc_ref = refs[8:]
    own, xi, yi = coords[0], coords[1], coords[2]
    cap, width = q_ref.shape
    heads = width // HEAD_DIM
    factor = LOG2E / math.sqrt(HEAD_DIM)

    row = lax.broadcasted_iota(jnp.int32, (cap, HEAD_DIM), 0)
    for k in range(4):
        for j in range(4):
            for half in range(2):
                at = (j * 2 + half) * cap
                shard = half * 16 + j * 4 + ring_index(yi - k)
                keys[pl.ds(pl.multiple_of(shard * cap, cap), cap), :] = k_refs[k][at : at + cap, :]
                shard = half * 16 + ring_index(xi - k) * 4 + j
                live = row < counts[shard]
                v = jnp.where(live, v_refs[k][at : at + cap, :].astype(F32), 0.0).astype(BF)
                spot = pl.ds(pl.multiple_of(shard * cap, cap), cap)
                vals[spot, :HEAD_DIM] = v
                vals[spot, HEAD_DIM:] = jnp.where(live, 1.0, 0.0).astype(BF)

    peak_ref[...] = jnp.full(peak_ref.shape, -1e30, F32)
    acc_ref[...] = jnp.zeros(acc_ref.shape, F32)
    first_own = own * cap

    def block(index, masked):
        start = pl.multiple_of(index * kb, kb)
        key_part = keys[pl.ds(start, kb), :]
        val_part = vals[pl.ds(start, kb), :]
        if masked:
            rows = lax.broadcasted_iota(jnp.int32, (cap, kb), 0)
            cols = lax.broadcasted_iota(jnp.int32, (cap, kb), 1)
            allowed = cols - rows <= first_own - start
        for h in range(heads):
            q = q_ref[:, h * HEAD_DIM : (h + 1) * HEAD_DIM]
            s = lax.dot_general(
                q, key_part, (((1,), (1,)), ((), ())), preferred_element_type=F32
            )
            if masked:
                s = jnp.where(allowed, s, -1e30)
            old = peak_ref[h]
            new = jnp.maximum(old, jnp.max(s, axis=1, keepdims=True))
            peak_ref[h] = new
            w = jnp.exp2((s - new[:, :1]) * factor).astype(BF)
            scale = jnp.exp2((old - new) * factor)
            acc_ref[h] = acc_ref[h] * jnp.concatenate([scale, scale], axis=1) + jnp.dot(
                w, val_part, preferred_element_type=F32
            )

    full = lax.div(first_own, kb)
    last = lax.div(first_own + (cap + kb - 1), kb)

    def plain(i, carry):
        block(i, False)
        return carry

    def edge(i, carry):
        block(i, True)
        return carry

    lax.fori_loop(0, full, plain, 0)
    lax.fori_loop(full, last, edge, 0)
    for h in range(heads):
        a = acc_ref[h]
        out_ref[:, h * HEAD_DIM : (h + 1) * HEAD_DIM] = (
            a[:, :HEAD_DIM] / a[:, HEAD_DIM:]
        ).astype(BF)


def out_body(coords, a_ref, w_ref, keep_ref, send_ref):
    zi, core = coords[3], coords[4]
    a = a_ref[...]
    for m in range(4):
        for mine in (True, False):
            owner = ring_index(zi + m) * 2 + (core if mine else 1 - core)
            half = lax.shift_right_logical(owner, 2)
            x = ring_index(owner)
            w = jnp.concatenate([w_ref[x, y, half] for y in range(4)], axis=1)
            part = jnp.dot(a, w, preferred_element_type=F32)
            if mine:
                keep_ref[m] = part
            else:
                send_ref[m] = part.astype(BF)


def place_body(coords, counts, kept_ref, hidden_ref, picked_ref, p0, p1, p2, p3, out_ref):
    ctx = coords[0]
    wanted = kept_ref[pl.ds(ctx, 1), :]
    count = hidden_ref.shape[0]
    cap = wanted.shape[1]
    projected = p0[...].astype(F32) + p1[...].astype(F32) + p2[...].astype(F32) + p3[...].astype(F32)
    updated = (picked_ref[...].astype(F32) + projected).astype(BF)
    place = lax.broadcasted_iota(jnp.int32, (count, cap), 0)
    slot = lax.broadcasted_iota(jnp.int32, (count, cap), 1)
    chosen = jnp.where((place == wanted) & (slot < counts[ctx]), 1.0, 0.0)
    replaced = jnp.sum(chosen, axis=1, keepdims=True) > 0.5
    moved = jnp.dot(chosen.astype(BF), updated, preferred_element_type=F32)
    out_ref[...] = jnp.where(replaced, moved, hidden_ref[...].astype(F32)).astype(BF)


def gather_xy(block):
    core = lax.axis_index("c")
    place = jnp.where(core == 0, lax.axis_index("x"), lax.axis_index("y"))
    got = [block] + [hop_mixed(block, True, k) for k in (1, 3, 2)]
    got = [got[0], got[1], got[3], got[2]]
    line = jnp.stack([got[0], got[3], got[2], got[1]] * 2)
    line = lax.dynamic_slice_in_dim(line, lax.rem(4 - place, 4), 4, 0)
    line = line.reshape((4 * block.shape[0],) + block.shape[1:])
    far = [hop_mixed(line, False, k) for k in (1, 3, 2)]
    return [line, far[0], far[2], far[1]]


def with_half(block):
    other = hop(block, "zh", 1)
    upper = lax.axis_index("zh") == 1
    return jnp.concatenate(
        [jnp.where(upper, other, block), jnp.where(upper, block, other)], axis=0
    )


def per_device(hidden, norm_gain, w_query, w_key, w_value, w_out, kept_rows, kept_count):
    cap = kept_rows.shape[1]
    heads = w_query.shape[1] // HEAD_DIM
    zh, x, y, zl, core = (lax.axis_index(a) for a in AXES)
    ctx = zh * 16 + x * 4 + y
    coords = jnp.stack([ctx, x, y, zl, core]).astype(jnp.int32)

    picked = pl.pallas_call(
        pick_body,
        out_shape=jax.ShapeDtypeStruct((cap, hidden.shape[1]), BF),
        in_specs=[SMEM, VMEM, VMEM],
        out_specs=VMEM,
    )(coords, kept_rows, hidden)

    w_kv = jnp.where(
        core == 0,
        lax.dynamic_slice_in_dim(w_key, zl * HEAD_DIM, HEAD_DIM, 1),
        lax.dynamic_slice_in_dim(w_value, zl * HEAD_DIM, HEAD_DIM, 1),
    )
    weights = gather_xy(with_half(jnp.concatenate([w_query, w_kv], axis=1)))

    pieces = jnp.stack([picked, hop(picked, "zl", 1), hop(picked, "zl", 2), hop(picked, "zl", 3)])
    others = hop(pieces, "c", 1)

    out_weights = lax.all_gather(w_out, "zh", axis=0)
    out_weights = lax.all_gather(out_weights, "y", axis=0)
    out_weights = lax.all_gather(out_weights, "x", axis=0)

    own_rows = lax.dynamic_index_in_dim(kept_rows, ctx, 0, keepdims=False)
    own_pos = ctx * hidden.shape[0] + own_rows
    exponent = jnp.arange(HEAD_DIM // 2, dtype=F32) * (2.0 / HEAD_DIM)
    inverse = jnp.exp(-math.log(ROPE_BASE) * exponent)
    angles = own_pos.astype(F32)[:, None] * inverse[None, :]
    cosine, sine = jnp.cos(angles), jnp.sin(angles)
    cosine = jnp.concatenate([cosine, cosine], axis=1)
    sine = jnp.concatenate([-sine, sine], axis=1)

    queries, own_kv = pl.pallas_call(
        project_body,
        out_shape=[
            jax.ShapeDtypeStruct((cap, heads * HEAD_DIM), BF),
            jax.ShapeDtypeStruct((cap, HEAD_DIM), BF),
        ],
        in_specs=[SMEM] + [VMEM] * 9,
        out_specs=[VMEM, VMEM],
        scratch_shapes=[pltpu.VMEM((4, cap, 1024), BF)],
        compiler_params=PARAMS,
    )(coords, pieces, others, norm_gain.reshape(1, -1), cosine, sine, *weights)

    mine = gather_xy(with_half(own_kv))
    theirs = [hop(part, "c", 1) for part in mine]
    key_parts = [jnp.where(core == 0, a, b) for a, b in zip(mine, theirs)]
    val_parts = [jnp.where(core == 0, b, a) for a, b in zip(mine, theirs)]

    slots = kept_rows.shape[0] * cap
    attended = pl.pallas_call(
        functools.partial(attend_body, 2048),
        out_shape=jax.ShapeDtypeStruct((cap, heads * HEAD_DIM), BF),
        in_specs=[SMEM, SMEM] + [VMEM] * 9,
        out_specs=VMEM,
        scratch_shapes=[
            pltpu.VMEM((slots, HEAD_DIM), BF),
            pltpu.VMEM((slots, 2 * HEAD_DIM), BF),
            pltpu.VMEM((heads, cap, HEAD_DIM), F32),
            pltpu.VMEM((heads, cap, 2 * HEAD_DIM), F32),
        ],
        compiler_params=PARAMS,
    )(coords, kept_count, queries, *key_parts, *val_parts)

    keep, send = pl.pallas_call(
        out_body,
        out_shape=[
            jax.ShapeDtypeStruct((4, cap, hidden.shape[1]), F32),
            jax.ShapeDtypeStruct((4, cap, hidden.shape[1]), BF),
        ],
        in_specs=[SMEM, VMEM, VMEM],
        out_specs=[VMEM, VMEM],
        compiler_params=PARAMS,
    )(coords, attended, out_weights)
    chip = (keep + hop(send, "c", 1).astype(F32)).astype(BF)
    parts = [chip[0]] + [hop(chip[m], "zl", m) for m in (1, 2, 3)]

    return pl.pallas_call(
        place_body,
        out_shape=jax.ShapeDtypeStruct(hidden.shape, BF),
        in_specs=[SMEM, SMEM] + [VMEM] * 7,
        out_specs=VMEM,
    )(coords, kept_count, kept_rows, hidden, picked, *parts)


def solution(mesh):
    ctx, tp = AXES[:3], AXES[3:]
    return jax.shard_map(
        per_device,
        mesh=Mesh(mesh.devices.reshape(SIZES), AXES),
        in_specs=(
            P(ctx, tp),
            P(),
            P(ctx, tp),
            P(ctx, None),
            P(ctx, None),
            P(tp, ctx),
            P(),
            P(),
        ),
        out_specs=P(ctx, tp),
        check_vma=False,
    )
```

time: 704 us -> 234 us (0.33); the launches traced: 696 us -> 234 us
  waiting for transfers between devices: 562 us -> 87.1 us
  matrix products: 75.4 us -> 0 us
  starting transfers between devices: 0.29 us -> 70 us
  Pallas kernels: 0 us -> 38.2 us
  other arithmetic: 31.5 us -> 5.37 us
  blocking collectives: 0 us -> 16.5 us
  local copies, waits for them, and re-layouts: 11.6 us -> 2.7 us
    all_gather x7 -> x2, waiting for transfers between devices: 522 us -> 20.3 us  [the longest x1 20.3 us: per_device(): out_weights = lax.all_gather(out_weights, 'y', axis=0)]
    dot_general x34 -> x0, matrix products: 75.4 us -> none  [the longest x15 31.6 us: accumulate(): jnp.einsum('rhgk,khd->rhgd', weights.astype(jnp.bfloat16), value_piece, p...]
    ppermute x0 -> x26, starting transfers between devices: none -> 69.9 us  [the longest x14 51.1 us: hop(): lax.ppermute(value, axis, [(i, (i + step) % size) for i in range(size)])]
    ppermute x0 -> x26, waiting for transfers between devices: none -> 66.8 us  [the longest x14 52.2 us: hop(): lax.ppermute(value, axis, [(i, (i + step) % size) for i in range(size)])]
    reduce_scatter x1 -> x0, waiting for transfers between devices: 39.1 us -> none  [per_device(): lax.psum_scatter(partial_out.astype(jnp.bfloat16), 'tp', scatter_dimensio...]
    pallas_call x0 -> x5, Pallas kernels: none -> 38.2 us  [the longest x1 22.8 us: per_device(): pl.pallas_call(functools.partial(attend_body, 2048), out_shape=jax.ShapeD...]
    reduce_sum x16 -> x0, other arithmetic: 19.2 us -> none  [the longest x15 16.8 us: accumulate(): row_total = row_total * rescale + jnp.sum(weights, axis=-1)]
    all_gather x0 -> x1, blocking collectives: none -> 16.5 us  [per_device(): out_weights = lax.all_gather(w_out, 'zh', axis=0)]
  transfers between devices with their start and end apart: 8 -> 28, of which waited for: 8 -> 14; matrix products, arithmetic and copies ran while one was open for 15% -> 2% of each run, Pallas kernels for 0% -> 13%
where the time goes in v1:
time: 234 us
  waiting for transfers between devices  87.1 us (37%)
  starting transfers between devices  70 us (30%)
  Pallas kernels  38.2 us (16%)
  blocking collectives  16.5 us (7%)
  between operations  13.8 us (6%)
  other arithmetic  5.37 us (2%)
  local copies, waits for them, and re-layouts  2.7 us (1%)
    ppermute x14, waiting for transfers between devices, hop(): lax.ppermute(value, axis, [(i, (i + step) % size) for i in range(size)])  52.2 us
    ppermute x14, starting transfers between devices, hop(): lax.ppermute(value, axis, [(i, (i + step) % size) for i in range(size)])  51.1 us
    pallas_call x1, Pallas kernels, per_device(): pl.pallas_call(functools.partial(attend_body, 2048), out_shape=jax.ShapeD...  22.8 us
    all_gather x1, waiting for transfers between devices, per_device(): out_weights = lax.all_gather(out_weights, 'y', axis=0)  20.3 us
    ppermute x12, starting transfers between devices, hop_mixed(): return lax.ppermute(value, ('x', 'y', 'c'), pairs)  18.8 us
    all_gather x1, blocking collectives, per_device(): out_weights = lax.all_gather(w_out, 'zh', axis=0)  16.5 us
    ppermute x12, waiting for transfers between devices, hop_mixed(): return lax.ppermute(value, ('x', 'y', 'c'), pairs)  14.6 us
    pallas_call x1, Pallas kernels, per_device(): pl.pallas_call(project_body, out_shape=[jax.ShapeDtypeStruct((cap, heads...  6.53 us
  transfers between devices with their start and end apart: 28, of which 14 were waited for; matrix products, arithmetic and copies ran while one was open for 2% of the time, Pallas kernels for 13%

profile of v1, /device:TPU:167, one launch (start us, length us, event | category | flops | bytes accessed | tf_op | source)
XLA Modules:
  0.0 233.7 jit_solution(2884777858919549352)
XLA Ops:
  6.5 0.8 dynamic-slice_select_fusion
  7.4 1.0 pad_maximum_fusion.4
  8.3 0.1 collective-permute-start.4
  8.5 0.6 stack.76.coords
  9.0 2.2 shard_map.82.picked_ref
  11.2 1.0 collective-permute-start
  12.2 1.8 collective-permute-start.1
  14.0 1.0 collective-permute-start.2
  15.0 5.7 %collective-permute-done.4 = bf16[128,640]{1,0:T(8,128)(2,1)S(1)} collective-permute-done((bf16[128,640]{1,0:T(8,128)(2,1)S(1)}, bf16[128,640]{1,0:T(8,128)(2,1)S(1)}, u32[]{:S(2)}, u32[]{:S(2)}) %collective-permute-start.4) | collective-permute-done | bytes 163872 | tf_op jit(solution)/shard_map/ppermute | solution.py:29
  20.7 0.1 broadcast_select_fusion.9
  20.7 0.8 pad_maximum_fusion.1
  21.5 2.7 %collective-permute-start.5 = (bf16[256,640]{1,0:T(8,128)(2,1)}, bf16[256,640]{1,0:T(8,128)(2,1)S(1)}, u32[]{:S(2)}, u32[]{:S(2)}) collective-permute-start(bf16[256,640]{1,0:T(8,128)(2,1)} %pad_maximum_fusion.1), channel_id=1, source_target_pairs={{0,96},{1,25},{8,104},{9,1},{16,112},{17,9},{24,120},{25,17},{32,0... | collective-permute-start | bytes 983048 | tf_op jit(solution)/shard_map/ppermute | solution.py:42
  24.2 16.5 %all-gather = bf16[1024,128]{1,0:T(8,128)(2,1)} all-gather(bf16[512,128]{1,0:T(8,128)(2,1)S(1)} %copy-done.8), channel_id=2, replica_groups=mesh['zh'=2,'x'=4,'y'=4,'zl'=4,'c'=2] {'zh'}, dimensions={0}, use_global_device_ids=true | all-gather | bytes 393216 | tf_op jit(solution)/shard_map/all_gather | solution.py:249
  40.7 0.0 all-gather.6.cloned.1.call-update
  40.7 0.0 all-gather.8.cloned.1.call-start
  40.8 3.0 %collective-permute-start.6 = (bf16[256,640]{1,0:T(8,128)(2,1)}, bf16[256,640]{1,0:T(8,128)(2,1)S(1)}, u32[]{:S(2)}, u32[]{:S(2)}) collective-permute-start(bf16[256,640]{1,0:T(8,128)(2,1)} %pad_maximum_fusion.1), channel_id=1, source_target_pairs={{0,64},{1,17},{8,72},{9,25},{16,80},{17,1},{24,88},{25,9},{32,96},... | collective-permute-start | bytes 983048 | tf_op jit(solution)/shard_map/ppermute | solution.py:42
  43.8 0.5 collective-permute-start.7
  44.3 5.1 %collective-permute-done.1 = bf16[320,512]{1,0:T(8,128)(2,1)S(1)} collective-permute-done((bf16[320,512]{1,0:T(8,128)(2,1)}, bf16[320,512]{1,0:T(8,128)(2,1)S(1)}, u32[]{:S(2)}, u32[]{:S(2)}) %collective-permute-start.1) | collective-permute-done | bytes 327712 | tf_op jit(solution)/shard_map/ppermute | solution.py:29
  49.4 3.3 %collective-permute-done.2 = bf16[320,512]{1,0:T(8,128)(2,1)S(1)} collective-permute-done((bf16[320,512]{1,0:T(8,128)(2,1)}, bf16[320,512]{1,0:T(8,128)(2,1)S(1)}, u32[]{:S(2)}, u32[]{:S(2)}) %collective-permute-start.2) | collective-permute-done | bytes 327712 | tf_op jit(solution)/shard_map/ppermute | solution.py:29
  52.7 0.2 pad_maximum_fusion.f_ref
  52.9 0.6 collective-permute-start.3
  53.9 0.1 constant_dynamic-slice_fusion
  54.0 0.6 collective-permute-start.10
  54.6 2.1 collective-permute-start.8
  56.8 20.3 %all-gather.6.cloned.1.call-done = bf16[8,512,128]{2,1,0:T(8,128)(2,1)} async-done(((bf16[2,512,128]{2,1,0:T(8,128)(2,1)}), bf16[8,512,128]{2,1,0:T(8,128)(2,1)}) %all-gather.6.cloned.1.call-update) | async-done | bytes 1048592 | tf_op jit(solution)/shard_map/all_gather | solution.py:250
  77.1 0.7 convert_reduce_fusion
  77.8 0.7 fusion
  78.5 0.2 pad_maximum_fusion.2
  78.7 8.0 %collective-permute-done.10.t3 = bf16[1024,640]{1,0:T(8,128)(2,1)} collective-permute-done((bf16[1024,640]{1,0:T(8,128)(2,1)S(1)}, bf16[1024,640]{1,0:T(8,128)(2,1)}, u32[]{:S(2)}, u32[]{:S(2)}) %collective-permute-start.10) | collective-permute-done | bytes 1310752 | tf_op jit(solution)/shard_map/ppermute | solution.py:42
  86.7 6.5 %shard_map.83 = (bf16[320,512]{1,0:T(8,128)(2,1)S(1)}, bf16[320,128]{1,0:T(8,128)(2,1)S(1)}) custom-call(s32[5]{0:T(128)S(1)} %copy-done, bf16[4,320,512]{2,1,0:T(8,128)(2,1)S(1)} %pad_maximum_fusion.f_ref, bf16[4,320,512]{2,1,0:T(8,128)(2,1)} %collective-permute-done.3.g_ref, f32[1,4096]{1,0:T(1,128)S(1)} %bitcast.53, ...), custom_call_target="tpu_custom_call" | custom-call | tf_op jit(solution)/shard_map/pallas_call | solution.py:262
  93.3 2.5 %collective-permute-start.11 = (bf16[320,128]{1,0:T(8,128)(2,1)S(1)}, bf16[320,128]{1,0:T(8,128)(2,1)S(1)}, u32[]{:S(2)}, u32[]{:S(2)}) collective-permute-start(bf16[320,128]{1,0:T(8,128)(2,1)S(1)} %get-tuple-element.10), channel_id=1, source_target_pairs={{0,128},{128,0},{1,129},{129,1},{2,130},{130,2},{3,131},{131,3},{4... | collective-permute-start | bytes 245768 | tf_op jit(solution)/shard_map/ppermute | solution.py:29
  95.8 4.8 %collective-permute-done.11 = bf16[320,128]{1,0:T(8,128)(2,1)S(1)} collective-permute-done((bf16[320,128]{1,0:T(8,128)(2,1)S(1)}, bf16[320,128]{1,0:T(8,128)(2,1)S(1)}, u32[]{:S(2)}, u32[]{:S(2)}) %collective-permute-start.11) | collective-permute-done | bytes 81952 | tf_op jit(solution)/shard_map/ppermute | solution.py:29
  100.6 2.5 %collective-permute-start.12 = (bf16[640,128]{1,0:T(8,128)(2,1)S(1)}, bf16[640,128]{1,0:T(8,128)(2,1)S(1)}, u32[]{:S(2)}, u32[]{:S(2)}) collective-permute-start(bf16[640,128]{1,0:T(8,128)(2,1)S(1)} %pad_maximum_fusion.5), channel_id=1, source_target_pairs={{0,96},{1,25},{8,104},{9,1},{16,112},{17,9},{24,120},{25,17},{32,0... | collective-permute-start | bytes 491528 | tf_op jit(solution)/shard_map/ppermute | solution.py:42
  103.1 0.4 collective-permute-start.13
  103.5 0.8 collective-permute-start.14
  104.3 2.8 %collective-permute-done.12 = bf16[640,128]{1,0:T(8,128)(2,1)S(1)} collective-permute-done((bf16[640,128]{1,0:T(8,128)(2,1)S(1)}, bf16[640,128]{1,0:T(8,128)(2,1)S(1)}, u32[]{:S(2)}, u32[]{:S(2)}) %collective-permute-start.12) | collective-permute-done | bytes 163872 | tf_op jit(solution)/shard_map/ppermute | solution.py:42
  107.1 1.7 collective-permute-done.13
  108.9 2.0 collective-permute-done.14
  111.1 0.1 constant_dynamic-slice_fusion.1
  111.1 3.7 %collective-permute-start.20 = (bf16[2560,128]{1,0:T(8,128)(2,1)S(1)}, bf16[2560,128]{1,0:T(8,128)(2,1)S(1)}, u32[]{:S(2)}, u32[]{:S(2)}) collective-permute-start(bf16[2560,128]{1,0:T(8,128)(2,1)S(1)} %bitcast.56), channel_id=1, source_target_pairs={{0,24},{1,97},{8,0},{9,105},{16,8},{17,113},{24,16},{25,121},{32,5... | collective-permute-start | bytes 1966088 | tf_op jit(solution)/shard_map/ppermute | solution.py:42
  114.8 1.0 collective-permute-start.18
  115.8 1.5 collective-permute-start.16
  117.3 23.6 %collective-permute-start.15 = (bf16[2560,128]{1,0:T(8,128)(2,1)S(1)}, bf16[2560,128]{1,0:T(8,128)(2,1)S(1)}, u32[]{:S(2)}, u32[]{:S(2)}) collective-permute-start(bf16[2560,128]{1,0:T(8,128)(2,1)S(1)} %bitcast.59), channel_id=1, source_target_pairs={{0,1},{1,0},{2,3},{3,2},{4,5},{5,4},{6,7},{7,6},{8,9},{9,8},{10,11... | collective-permute-start | bytes 1966088 | tf_op jit(solution)/shard_map/ppermute | solution.py:29
  140.9 8.2 %collective-permute-start.21 = (bf16[2560,128]{1,0:T(8,128)(2,1)S(1)}, bf16[2560,128]{1,0:T(8,128)(2,1)S(1)}, u32[]{:S(2)}, u32[]{:S(2)}) collective-permute-start(bf16[2560,128]{1,0:T(8,128)(2,1)S(1)} %collective-permute-done.20), channel_id=1, source_target_pairs={{0,1},{1,0},{2,3},{3,2},{4,5},{5,4},{6,7},{7,6},{8,9},{9,8},{10,11... | collective-permute-start | bytes 1966088 | tf_op jit(solution)/shard_map/ppermute | solution.py:29
  149.1 2.5 %collective-permute-start.19 = (bf16[2560,128]{1,0:T(8,128)(2,1)S(1)}, bf16[2560,128]{1,0:T(8,128)(2,1)S(1)}, u32[]{:S(2)}, u32[]{:S(2)}) collective-permute-start(bf16[2560,128]{1,0:T(8,128)(2,1)S(1)} %collective-permute-done.18), channel_id=1, source_target_pairs={{0,1},{1,0},{2,3},{3,2},{4,5},{5,4},{6,7},{7,6},{8,9},{9,8},{10,11... | collective-permute-start | bytes 1966088 | tf_op jit(solution)/shard_map/ppermute | solution.py:29
  151.6 6.9 %collective-permute-start.17 = (bf16[2560,128]{1,0:T(8,128)(2,1)S(1)}, bf16[2560,128]{1,0:T(8,128)(2,1)S(1)}, u32[]{:S(2)}, u32[]{:S(2)}) collective-permute-start(bf16[2560,128]{1,0:T(8,128)(2,1)S(1)} %collective-permute-done.16), channel_id=1, source_target_pairs={{0,1},{1,0},{2,3},{3,2},{4,5},{5,4},{6,7},{7,6},{8,9},{9,8},{10,11... | collective-permute-start | bytes 1966088 | tf_op jit(solution)/shard_map/ppermute | solution.py:29
  158.5 0.1 broadcast_select_fusion.3
  158.7 0.1 broadcast_select_fusion
  158.8 0.1 broadcast_select_fusion.1
  158.9 1.4 collective-permute-done.17
  160.3 0.1 broadcast_select_fusion.2
  160.4 22.8 %shard_map.84.a_ref = bf16[320,512]{1,0:T(8,128)(2,1)S(1)} custom-call(s32[5]{0:T(128)S(1)} %copy-done, s32[32]{0:T(128)S(1)} %copy-done.2, bf16[320,512]{1,0:T(8,128)(2,1)S(1)} %get-tuple-element.9.q_ref, bf16[2560,128]{1,0:T(8,128)(2,1)S(1)} %get-tuple-element.24.refs_0_, bf16[2560,128]{1,0:T(8,128)(2,1)S(1)} %get-tuple-element.22.refs_1_, ...), custom_call_target="tpu_custom_call" | custom-call | tf_op jit(solution)/shard_map/pallas_call | solution.py:280
  183.2 0.0 all-gather.8.cloned.1.call-done
  183.2 3.8 %shard_map.85 = (f32[4,320,512]{2,1,0:T(8,128)S(1)}, bf16[4,320,512]{2,1,0:T(8,128)(2,1)S(1)}) custom-call(s32[5]{0:T(128)S(1)} %copy-done, bf16[320,512]{1,0:T(8,128)(2,1)S(1)} %shard_map.84.a_ref, bf16[4,4,2,512,128]{4,3,2,1,0:T(8,128)(2,1)} %bitcast.54), custom_call_target="tpu_custom_call" | custom-call | tf_op jit(solution)/shard_map/pallas_call | solution.py:294
  187.0 0.7 collective-permute-start.22
  187.7 2.7 %collective-permute-done.22 = bf16[4,320,512]{2,1,0:T(8,128)(2,1)S(1)} collective-permute-done((bf16[4,320,512]{2,1,0:T(8,128)(2,1)S(1)}, bf16[4,320,512]{2,1,0:T(8,128)(2,1)S(1)}, u32[]{:S(2)}, u32[]{:S(2)}) %collective-permute-start.22) | collective-permute-done | bytes 1310752 | tf_op jit(solution)/shard_map/ppermute | solution.py:29
  190.4 0.5 add_convert_fusion
  190.9 0.8 slice_bitcast_fusion
  191.7 2.2 collective-permute-start.24
  193.9 6.7 %collective-permute-done.23.p1 = bf16[320,512]{1,0:T(8,128)(2,1)S(1)} collective-permute-done((bf16[320,512]{1,0:T(8,128)(2,1)S(1)}, bf16[320,512]{1,0:T(8,128)(2,1)S(1)}, u32[]{:S(2)}, u32[]{:S(2)}) %collective-permute-start.23) | collective-permute-done | bytes 327712 | tf_op jit(solution)/shard_map/ppermute | solution.py:29
  200.6 19.2 %collective-permute-done.24.p2 = bf16[320,512]{1,0:T(8,128)(2,1)S(1)} collective-permute-done((bf16[320,512]{1,0:T(8,128)(2,1)S(1)}, bf16[320,512]{1,0:T(8,128)(2,1)S(1)}, u32[]{:S(2)}, u32[]{:S(2)}) %collective-permute-start.24) | collective-permute-done | bytes 327712 | tf_op jit(solution)/shard_map/ppermute | solution.py:29
  219.8 3.4 %collective-permute-done.25.p3 = bf16[320,512]{1,0:T(8,128)(2,1)S(1)} collective-permute-done((bf16[320,512]{1,0:T(8,128)(2,1)S(1)}, bf16[320,512]{1,0:T(8,128)(2,1)S(1)}, u32[]{:S(2)}, u32[]{:S(2)}) %collective-permute-start.25) | collective-permute-done | bytes 327712 | tf_op jit(solution)/shard_map/ppermute | solution.py:29
  223.2 0.7 copy-done.7
  223.9 2.9 %shard_map.86 = bf16[512,512]{1,0:T(8,128)(2,1)} custom-call(s32[5]{0:T(128)} %stack.76.coords, s32[32]{0:T(128)} %counts.3, s32[32,320]{1,0:T(8,128)} %kept_ref.3, bf16[512,512]{1,0:T(8,128)(2,1)} %hidden_ref.3, bf16[320,512]{1,0:T(8,128)(2,1)} %shard_map.82.picked_ref, bf16[320,512]{1,0:T(8,128)(2,1)} %get-tuple-element.16.p0, bf16[320,512]{1,0:T(8,128)(2,1)} %copy-done.5, ...), custom_call_target="tpu_custom_call" | custom-call | tf_op jit(solution)/shard_map/pallas_call | solution.py:307
  (54 shorter events, 0.6 us)
Async XLA Ops:
  6.5 14.1 %copy-start.4 = (bf16[128,512]{1,0:T(8,128)(2,1)S(1)}, bf16[128,512]{1,0:T(8,128)(2,1)}, u32[]{:S(2)}) copy-start(bf16[128,512]{1,0:T(8,128)(2,1)} %param.10) | copy-start | bytes 393220
  6.5 70.5 %all-gather.6.cloned.1.call-start = ((), (), s32[]{:S(2)}) async-start(), calls=%async_computation | async-start | bytes 1310720 | tf_op jit(solution)/shard_map/all_gather | solution.py:250
  7.4 16.9 %copy-start.8 = (bf16[512,128]{1,0:T(8,128)(2,1)S(1)}, bf16[512,128]{1,0:T(8,128)(2,1)}, u32[]{:S(2)}) copy-start(bf16[512,128]{1,0:T(8,128)(2,1)} %param.13) | copy-start | bytes 393220
  8.3 12.3 %collective-permute-start.4 = (bf16[128,640]{1,0:T(8,128)(2,1)S(1)}, bf16[128,640]{1,0:T(8,128)(2,1)S(1)}, u32[]{:S(2)}, u32[]{:S(2)}) collective-permute-start(bf16[128,640]{1,0:T(8,128)(2,1)S(1)} %pad_maximum_fusion.4), channel_id=1, source_target_pairs={{0,128},{128,0},{1,129},{129,1},{2,130},{130,2},{3,131},{131,3},{4... | collective-permute-start | bytes 491528 | tf_op jit(solution)/shard_map/ppermute | solution.py:29
  11.2 32.6 %collective-permute-start = (bf16[320,512]{1,0:T(8,128)(2,1)}, bf16[320,512]{1,0:T(8,128)(2,1)S(1)}, u32[]{:S(2)}, u32[]{:S(2)}) collective-permute-start(bf16[320,512]{1,0:T(8,128)(2,1)} %shard_map.82.picked_ref), channel_id=1, source_target_pairs={{0,2},{2,4},{4,6},{6,0},{1,3},{3,5},{5,7},{7,1},{8,10},{10,12},{12... | collective-permute-start | bytes 983048 | tf_op jit(solution)/shard_map/ppermute | solution.py:29
  12.2 37.2 %collective-permute-start.1 = (bf16[320,512]{1,0:T(8,128)(2,1)}, bf16[320,512]{1,0:T(8,128)(2,1)S(1)}, u32[]{:S(2)}, u32[]{:S(2)}) collective-permute-start(bf16[320,512]{1,0:T(8,128)(2,1)} %shard_map.82.picked_ref), channel_id=1, source_target_pairs={{0,4},{2,6},{4,0},{6,2},{1,5},{3,7},{5,1},{7,3},{8,12},{10,14},{12... | collective-permute-start | bytes 983048 | tf_op jit(solution)/shard_map/ppermute | solution.py:29
  14.0 38.7 %collective-permute-start.2 = (bf16[320,512]{1,0:T(8,128)(2,1)}, bf16[320,512]{1,0:T(8,128)(2,1)S(1)}, u32[]{:S(2)}, u32[]{:S(2)}) collective-permute-start(bf16[320,512]{1,0:T(8,128)(2,1)} %shard_map.82.picked_ref), channel_id=1, source_target_pairs={{0,6},{2,0},{4,2},{6,4},{1,7},{3,1},{5,3},{7,5},{8,14},{10,8},{12,... | collective-permute-start | bytes 983048 | tf_op jit(solution)/shard_map/ppermute | solution.py:29
  15.0 37.8 %copy-start.3 = (bf16[320,512]{1,0:T(8,128)(2,1)S(1)}, bf16[320,512]{1,0:T(8,128)(2,1)}, u32[]{:S(2)}) copy-start(bf16[320,512]{1,0:T(8,128)(2,1)} %shard_map.82.picked_ref) | copy-start | bytes 983044
  21.5 32.0 %collective-permute-start.5 = (bf16[256,640]{1,0:T(8,128)(2,1)}, bf16[256,640]{1,0:T(8,128)(2,1)S(1)}, u32[]{:S(2)}, u32[]{:S(2)}) collective-permute-start(bf16[256,640]{1,0:T(8,128)(2,1)} %pad_maximum_fusion.1), channel_id=1, source_target_pairs={{0,96},{1,25},{8,104},{9,1},{16,112},{17,9},{24,120},{25,17},{32,0... | collective-permute-start | bytes 983048 | tf_op jit(solution)/shard_map/ppermute | solution.py:42
  40.7 142.5 %all-gather.8.cloned.1.call-start = ((), (), s32[]{:S(2)}) async-start(), calls=%async_computation.1 | async-start | bytes 5242880 | tf_op jit(solution)/shard_map/all_gather | solution.py:251
  40.8 12.7 %collective-permute-start.6 = (bf16[256,640]{1,0:T(8,128)(2,1)}, bf16[256,640]{1,0:T(8,128)(2,1)S(1)}, u32[]{:S(2)}, u32[]{:S(2)}) collective-permute-start(bf16[256,640]{1,0:T(8,128)(2,1)} %pad_maximum_fusion.1), channel_id=1, source_target_pairs={{0,64},{1,17},{8,72},{9,25},{16,80},{17,1},{24,88},{25,9},{32,96},... | collective-permute-start | bytes 983048 | tf_op jit(solution)/shard_map/ppermute | solution.py:42
  43.8 9.8 %collective-permute-start.7 = (bf16[256,640]{1,0:T(8,128)(2,1)}, bf16[256,640]{1,0:T(8,128)(2,1)S(1)}, u32[]{:S(2)}, u32[]{:S(2)}) collective-permute-start(bf16[256,640]{1,0:T(8,128)(2,1)} %pad_maximum_fusion.1), channel_id=1, source_target_pairs={{0,32},{1,9},{8,40},{9,17},{16,48},{17,25},{24,56},{25,1},{32,64},... | collective-permute-start | bytes 983048 | tf_op jit(solution)/shard_map/ppermute | solution.py:42
  52.9 25.8 %collective-permute-start.3 = (bf16[4,320,512]{2,1,0:T(8,128)(2,1)S(1)}, bf16[4,320,512]{2,1,0:T(8,128)(2,1)}, u32[]{:S(2)}, u32[]{:S(2)}) collective-permute-start(bf16[4,320,512]{2,1,0:T(8,128)(2,1)S(1)} %pad_maximum_fusion.f_ref), channel_id=1, source_target_pairs={{0,1},{1,0},{2,3},{3,2},{4,5},{5,4},{6,7},{7,6},{8,9},{9,8},{10,11... | collective-permute-start | bytes 3932168 | tf_op jit(solution)/shard_map/ppermute | solution.py:29
  54.0 32.7 %copy-start = (s32[5]{0:T(128)S(1)}, s32[5]{0:T(128)}, u32[]{:S(2)}) copy-start(s32[5]{0:T(128)} %stack.76.coords) | copy-start | bytes 64
  54.0 32.7 %copy-start.1 = (f32[4096]{0:T(1024)S(1)}, f32[4096]{0:T(1024)}, u32[]{:S(2)}) copy-start(f32[4096]{0:T(1024)} %param.9) | copy-start | bytes 49156
  54.0 32.7 %collective-permute-start.10 = (bf16[1024,640]{1,0:T(8,128)(2,1)S(1)}, bf16[1024,640]{1,0:T(8,128)(2,1)}, u32[]{:S(2)}, u32[]{:S(2)}) collective-permute-start(bf16[1024,640]{1,0:T(8,128)(2,1)S(1)} %bitcast.49), channel_id=1, source_target_pairs={{0,24},{1,97},{8,0},{9,105},{16,8},{17,113},{24,16},{25,121},{32,5... | collective-permute-start | bytes 3932168 | tf_op jit(solution)/shard_map/ppermute | solution.py:42
  54.6 32.1 %collective-permute-start.8 = (bf16[1024,640]{1,0:T(8,128)(2,1)S(1)}, bf16[1024,640]{1,0:T(8,128)(2,1)}, u32[]{:S(2)}, u32[]{:S(2)}) collective-permute-start(bf16[1024,640]{1,0:T(8,128)(2,1)S(1)} %bitcast.50), channel_id=1, source_target_pairs={{0,8},{1,33},{8,16},{9,41},{16,24},{17,49},{24,0},{25,57},{32,40},... | collective-permute-start | bytes 3932168 | tf_op jit(solution)/shard_map/ppermute | solution.py:42
  56.8 29.9 %collective-permute-start.9 = (bf16[1024,640]{1,0:T(8,128)(2,1)S(1)}, bf16[1024,640]{1,0:T(8,128)(2,1)}, u32[]{:S(2)}, u32[]{:S(2)}) collective-permute-start(bf16[1024,640]{1,0:T(8,128)(2,1)S(1)} %bitcast.51), channel_id=1, source_target_pairs={{0,16},{1,65},{8,24},{9,73},{16,0},{17,81},{24,8},{25,89},{32,48},... | collective-permute-start | bytes 3932168 | tf_op jit(solution)/shard_map/ppermute | solution.py:42
  93.3 7.3 %collective-permute-start.11 = (bf16[320,128]{1,0:T(8,128)(2,1)S(1)}, bf16[320,128]{1,0:T(8,128)(2,1)S(1)}, u32[]{:S(2)}, u32[]{:S(2)}) collective-permute-start(bf16[320,128]{1,0:T(8,128)(2,1)S(1)} %get-tuple-element.10), channel_id=1, source_target_pairs={{0,128},{128,0},{1,129},{129,1},{2,130},{130,2},{3,131},{131,3},{4... | collective-permute-start | bytes 245768 | tf_op jit(solution)/shard_map/ppermute | solution.py:29
  100.6 6.5 %collective-permute-start.12 = (bf16[640,128]{1,0:T(8,128)(2,1)S(1)}, bf16[640,128]{1,0:T(8,128)(2,1)S(1)}, u32[]{:S(2)}, u32[]{:S(2)}) collective-permute-start(bf16[640,128]{1,0:T(8,128)(2,1)S(1)} %pad_maximum_fusion.5), channel_id=1, source_target_pairs={{0,96},{1,25},{8,104},{9,1},{16,112},{17,9},{24,120},{25,17},{32,0... | collective-permute-start | bytes 491528 | tf_op jit(solution)/shard_map/ppermute | solution.py:42
  103.1 5.8 %collective-permute-start.13 = (bf16[640,128]{1,0:T(8,128)(2,1)S(1)}, bf16[640,128]{1,0:T(8,128)(2,1)S(1)}, u32[]{:S(2)}, u32[]{:S(2)}) collective-permute-start(bf16[640,128]{1,0:T(8,128)(2,1)S(1)} %pad_maximum_fusion.5), channel_id=1, source_target_pairs={{0,64},{1,17},{8,72},{9,25},{16,80},{17,1},{24,88},{25,9},{32,96},... | collective-permute-start | bytes 491528 | tf_op jit(solution)/shard_map/ppermute | solution.py:42
  103.5 7.4 %collective-permute-start.14 = (bf16[640,128]{1,0:T(8,128)(2,1)S(1)}, bf16[640,128]{1,0:T(8,128)(2,1)S(1)}, u32[]{:S(2)}, u32[]{:S(2)}) collective-permute-start(bf16[640,128]{1,0:T(8,128)(2,1)S(1)} %pad_maximum_fusion.5), channel_id=1, source_target_pairs={{0,32},{1,9},{8,40},{9,17},{16,48},{17,25},{24,56},{25,1},{32,64},... | collective-permute-start | bytes 491528 | tf_op jit(solution)/shard_map/ppermute | solution.py:42
  111.1 29.8 %collective-permute-start.20 = (bf16[2560,128]{1,0:T(8,128)(2,1)S(1)}, bf16[2560,128]{1,0:T(8,128)(2,1)S(1)}, u32[]{:S(2)}, u32[]{:S(2)}) collective-permute-start(bf16[2560,128]{1,0:T(8,128)(2,1)S(1)} %bitcast.56), channel_id=1, source_target_pairs={{0,24},{1,97},{8,0},{9,105},{16,8},{17,113},{24,16},{25,121},{32,5... | collective-permute-start | bytes 1966088 | tf_op jit(solution)/shard_map/ppermute | solution.py:42
  114.8 34.3 %collective-permute-start.18 = (bf16[2560,128]{1,0:T(8,128)(2,1)S(1)}, bf16[2560,128]{1,0:T(8,128)(2,1)S(1)}, u32[]{:S(2)}, u32[]{:S(2)}) collective-permute-start(bf16[2560,128]{1,0:T(8,128)(2,1)S(1)} %bitcast.57), channel_id=1, source_target_pairs={{0,16},{1,65},{8,24},{9,73},{16,0},{17,81},{24,8},{25,89},{32,48},... | collective-permute-start | bytes 1966088 | tf_op jit(solution)/shard_map/ppermute | solution.py:42
  115.8 35.8 %collective-permute-start.16 = (bf16[2560,128]{1,0:T(8,128)(2,1)S(1)}, bf16[2560,128]{1,0:T(8,128)(2,1)S(1)}, u32[]{:S(2)}, u32[]{:S(2)}) collective-permute-start(bf16[2560,128]{1,0:T(8,128)(2,1)S(1)} %bitcast.58), channel_id=1, source_target_pairs={{0,8},{1,33},{8,16},{9,41},{16,24},{17,49},{24,0},{25,57},{32,40},... | collective-permute-start | bytes 1966088 | tf_op jit(solution)/shard_map/ppermute | solution.py:42
  117.3 41.2 %collective-permute-start.15 = (bf16[2560,128]{1,0:T(8,128)(2,1)S(1)}, bf16[2560,128]{1,0:T(8,128)(2,1)S(1)}, u32[]{:S(2)}, u32[]{:S(2)}) collective-permute-start(bf16[2560,128]{1,0:T(8,128)(2,1)S(1)} %bitcast.59), channel_id=1, source_target_pairs={{0,1},{1,0},{2,3},{3,2},{4,5},{5,4},{6,7},{7,6},{8,9},{9,8},{10,11... | collective-permute-start | bytes 1966088 | tf_op jit(solution)/shard_map/ppermute | solution.py:29
  140.9 17.7 %collective-permute-start.21 = (bf16[2560,128]{1,0:T(8,128)(2,1)S(1)}, bf16[2560,128]{1,0:T(8,128)(2,1)S(1)}, u32[]{:S(2)}, u32[]{:S(2)}) collective-permute-start(bf16[2560,128]{1,0:T(8,128)(2,1)S(1)} %collective-permute-done.20), channel_id=1, source_target_pairs={{0,1},{1,0},{2,3},{3,2},{4,5},{5,4},{6,7},{7,6},{8,9},{9,8},{10,11... | collective-permute-start | bytes 1966088 | tf_op jit(solution)/shard_map/ppermute | solution.py:29
  149.1 9.6 %collective-permute-start.19 = (bf16[2560,128]{1,0:T(8,128)(2,1)S(1)}, bf16[2560,128]{1,0:T(8,128)(2,1)S(1)}, u32[]{:S(2)}, u32[]{:S(2)}) collective-permute-start(bf16[2560,128]{1,0:T(8,128)(2,1)S(1)} %collective-permute-done.18), channel_id=1, source_target_pairs={{0,1},{1,0},{2,3},{3,2},{4,5},{5,4},{6,7},{7,6},{8,9},{9,8},{10,11... | collective-permute-start | bytes 1966088 | tf_op jit(solution)/shard_map/ppermute | solution.py:29
  151.6 8.6 %collective-permute-start.17 = (bf16[2560,128]{1,0:T(8,128)(2,1)S(1)}, bf16[2560,128]{1,0:T(8,128)(2,1)S(1)}, u32[]{:S(2)}, u32[]{:S(2)}) collective-permute-start(bf16[2560,128]{1,0:T(8,128)(2,1)S(1)} %collective-permute-done.16), channel_id=1, source_target_pairs={{0,1},{1,0},{2,3},{3,2},{4,5},{5,4},{6,7},{7,6},{8,9},{9,8},{10,11... | collective-permute-start | bytes 1966088 | tf_op jit(solution)/shard_map/ppermute | solution.py:29
  158.9 1.5 copy-start.2
  187.0 3.4 %collective-permute-start.22 = (bf16[4,320,512]{2,1,0:T(8,128)(2,1)S(1)}, bf16[4,320,512]{2,1,0:T(8,128)(2,1)S(1)}, u32[]{:S(2)}, u32[]{:S(2)}) collective-permute-start(bf16[4,320,512]{2,1,0:T(8,128)(2,1)S(1)} %get-tuple-element.12), channel_id=1, source_target_pairs={{0,1},{1,0},{2,3},{3,2},{4,5},{5,4},{6,7},{7,6},{8,9},{9,8},{10,11... | collective-permute-start | bytes 3932168 | tf_op jit(solution)/shard_map/ppermute | solution.py:29
  191.7 8.9 %collective-permute-start.23 = (bf16[320,512]{1,0:T(8,128)(2,1)S(1)}, bf16[320,512]{1,0:T(8,128)(2,1)S(1)}, u32[]{:S(2)}, u32[]{:S(2)}) collective-permute-start(bf16[320,512]{1,0:T(8,128)(2,1)S(1)} %get-tuple-element.15), channel_id=1, source_target_pairs={{0,2},{2,4},{4,6},{6,0},{1,3},{3,5},{5,7},{7,1},{8,10},{10,12},{12... | collective-permute-start | bytes 983048 | tf_op jit(solution)/shard_map/ppermute | solution.py:29
  191.7 28.1 %collective-permute-start.24 = (bf16[320,512]{1,0:T(8,128)(2,1)S(1)}, bf16[320,512]{1,0:T(8,128)(2,1)S(1)}, u32[]{:S(2)}, u32[]{:S(2)}) collective-permute-start(bf16[320,512]{1,0:T(8,128)(2,1)S(1)} %get-tuple-element.14), channel_id=1, source_target_pairs={{0,4},{2,6},{4,0},{6,2},{1,5},{3,7},{5,1},{7,3},{8,12},{10,14},{12... | collective-permute-start | bytes 983048 | tf_op jit(solution)/shard_map/ppermute | solution.py:29
  193.9 29.3 %collective-permute-start.25 = (bf16[320,512]{1,0:T(8,128)(2,1)S(1)}, bf16[320,512]{1,0:T(8,128)(2,1)S(1)}, u32[]{:S(2)}, u32[]{:S(2)}) collective-permute-start(bf16[320,512]{1,0:T(8,128)(2,1)S(1)} %get-tuple-element.13), channel_id=1, source_target_pairs={{0,6},{2,0},{4,2},{6,4},{1,7},{3,1},{5,3},{7,5},{8,14},{10,8},{12,... | collective-permute-start | bytes 983048 | tf_op jit(solution)/shard_map/ppermute | solution.py:29
  200.6 22.6 %copy-start.5 = (bf16[320,512]{1,0:T(8,128)(2,1)}, bf16[320,512]{1,0:T(8,128)(2,1)S(1)}, u32[]{:S(2)}) copy-start(bf16[320,512]{1,0:T(8,128)(2,1)S(1)} %collective-permute-done.23.p1) | copy-start | bytes 983044
  219.8 3.4 %copy-start.6 = (bf16[320,512]{1,0:T(8,128)(2,1)}, bf16[320,512]{1,0:T(8,128)(2,1)S(1)}, u32[]{:S(2)}) copy-start(bf16[320,512]{1,0:T(8,128)(2,1)S(1)} %collective-permute-done.24.p2) | copy-start | bytes 983044
  223.2 0.7 copy-start.7
Sparse Core Ops, SparseCore 0:
  40.9 36.1 all-gather.5
  78.9 64.5 all-gather.7
